TPU v7x, 32 devices: a whole 2x2x4 slice. The times are simulated.
32 devices in a mesh: shard: 4 (over z), tensor: 4 (over y, x), section: 2 (over core).
Axes of the slice: x: 2, y: 2, z: 4, core: 2. Of those that a mesh axis runs over, the one named last changes fastest.
Arguments:
- gradient: bfloat16 [32, 512, 2048], P(('tensor', 'section'), 'shard'), may hold values from -48 to 48
- momentum: float32 [32, 512, 2048], P(('tensor', 'section'), 'shard'), may hold values from -8 to 8
- normed: bfloat16 [4096, 512], P(('shard', 'section'), 'tensor'), may hold values from -6 to 6
- ln_gain: float32 [512], P('tensor'), may hold values from 0.5 to 1.5
- ln_bias: float32 [512], P('tensor'), may hold values from -3 to 3
- ln_cotangent: bfloat16 [4096, 512], P(('shard', 'section'), 'tensor'), may hold values from -0.375 to 0.375
- router_cotangent: bfloat16 [4096, 32], P(('shard', 'section')), may hold values from -0.375 to 0.375
- first_moment: float32 [34, 512], P(None, 'tensor'), may hold values from -3 to 3
- second_moment: float32 [34, 512], P(None, 'tensor'), may hold values from 0.5 to 5
Outputs:
- next_momentum: float32 [32, 512, 2048], P(('tensor', 'section'), 'shard')
- update: float32 [32, 512, 2048], P(('tensor', 'section'), 'shard')
- next_first: float32 [34, 512], P(None, 'tensor')
- next_second: float32 [34, 512], P(None, 'tensor')
- adam_step: float32 [34, 512], P(None, 'tensor')
All inputs are finite; a program needn't handle non-finite values.
Results may differ from a plain program's by a relative error of at most 0.035.
Values may be sent and summed in bfloat16 or wider, within the bound.
A program may use at most 64 MiB of HBM per device.

v0:
```python
import math

import jax
import jax.numpy as jnp
from jax import lax
from jax.sharding import PartitionSpec as P

FF = 2048
ITERS = 5


MUON_DECAY = 0.95
LINEAR_TERM = 3.4445
CUBIC_TERM = -4.775
QUINTIC_TERM = 2.0315
NORM_EPSILON = 1e-07
ADAM_FIRST = 0.9
ADAM_SECOND = 0.95
ADAM_EPSILON = 1e-08


def keep_local(value):
    return value


def orthogonalize(blocks, join_sums, join_grams):
    squares = jnp.sum(jnp.square(blocks.astype(jnp.float32)), axis=(1, 2))
    total = jnp.sqrt(join_sums(squares))
    iterate = (blocks.astype(jnp.float32) / (total + NORM_EPSILON)[:, None, None]).astype(
        jnp.bfloat16
    )
    for repeat in range(ITERS):
        gram = join_grams(
            jnp.einsum("kij,klj->kil", iterate, iterate, preferred_element_type=jnp.float32)
        )
        gram_half = gram.astype(jnp.bfloat16)
        square_term = jnp.einsum(
            "kij,kjl->kil", gram_half, gram_half, preferred_element_type=jnp.float32
        )
        poly = (CUBIC_TERM * gram + QUINTIC_TERM * square_term).astype(jnp.bfloat16)
        product = jnp.einsum("kij,kjl->kil", poly, iterate, preferred_element_type=jnp.float32)
        iterate = (LINEAR_TERM * iterate.astype(jnp.float32) + product).astype(jnp.bfloat16)
    return iterate


def on_device(
    gradient,
    momentum,
    normed,
    ln_gain,
    ln_bias,
    ln_cotangent,
    router_cotangent,
    first_moment,
    second_moment,
):
    grad_float = gradient.astype(jnp.float32)
    next_momentum = MUON_DECAY * momentum + grad_float
    nesterov = (grad_float + MUON_DECAY * next_momentum).astype(jnp.bfloat16)
    count_all, rows_piece, cols_full = nesterov.shape
    shard_count = lax.axis_size("shard")
    normed_float = normed.astype(jnp.float32)
    cot_float = ln_cotangent.astype(jnp.float32)
    ln_out = (ln_gain[None, :] * normed_float + ln_bias[None, :]).astype(jnp.bfloat16)
    gain_local = jnp.sum(cot_float * normed_float, axis=0)
    bias_local = jnp.sum(cot_float, axis=0)
    router_local = lax.dot_general(
        router_cotangent, ln_out, (((0,), (0,)), ((), ())), preferred_element_type=jnp.float32
    )
    gain_grad, bias_grad, router_grad = lax.psum(
        (gain_local, bias_local, router_local), ("shard", "section")
    )
    vec_grad = jnp.concatenate([gain_grad[None, :], bias_grad[None, :], router_grad], axis=0)
    next_first = ADAM_FIRST * first_moment + (1.0 - ADAM_FIRST) * vec_grad
    next_second = ADAM_SECOND * second_moment + (1.0 - ADAM_SECOND) * vec_grad * vec_grad
    adam_step = next_first / (jnp.sqrt(next_second) + ADAM_EPSILON)
    slots = -(-count_all // shard_count)
    padded = jnp.pad(nesterov, ((0, slots * shard_count - count_all), (0, 0), (0, 0)))
    outgoing = padded.reshape(slots, shard_count, rows_piece, cols_full).transpose(1, 0, 2, 3)
    received = lax.all_to_all(outgoing, "shard", split_axis=0, concat_axis=0, tiled=True)
    items = received.shape[1]
    blocks = received.transpose(1, 0, 2, 3).reshape(items, shard_count * rows_piece, cols_full)
    result = orthogonalize(blocks, keep_local, keep_local)
    returned = lax.all_to_all(
        result.reshape(items, shard_count, rows_piece, cols_full).transpose(1, 0, 2, 3),
        "shard",
        split_axis=0,
        concat_axis=0,
        tiled=True,
    )
    ordered = returned.transpose(1, 0, 2, 3).reshape(slots * shard_count, rows_piece, cols_full)
    update = ordered[:count_all].astype(jnp.float32) * math.sqrt(FF)
    return (next_momentum, update, next_first, next_second, adam_step)


def solution(mesh):
    return jax.shard_map(
        on_device,
        mesh=mesh,
        in_specs=(
            P(("tensor", "section"), "shard", None),
            P(("tensor", "section"), "shard", None),
            P(("shard", "section"), "tensor"),
            P("tensor"),
            P("tensor"),
            P(("shard", "section"), "tensor"),
            P(("shard", "section"), None),
            P(None, "tensor"),
            P(None, "tensor"),
        ),
        out_specs=(
            P(("tensor", "section"), "shard", None),
            P(("tensor", "section"), "shard", None),
            P(None, "tensor"),
            P(None, "tensor"),
            P(None, "tensor"),
        ),
        check_vma=False,
    )
```

profile of v0, /device:TPU:1, one launch (start us, length us, event | category | flops | bytes accessed | tf_op | source)
XLA Modules:
  0.0 160.6 jit_solution(11884171841259081540)
XLA Ops:
  0.6 0.0 copy-start
  0.6 6.0 %fusion.3 = (bf16[4,1,128,2048]{3,2,1,0:T(8,128)(2,1)S(1)}, f32[4,128,2048]{2,1,0:T(8,128)}) fusion(bf16[4,128,2048]{2,1,0:T(8,128)(2,1)} %param.9, f32[4,128,2048]{2,1,0:T(8,128)} %param.10), kind=kLoop, calls=%fused_computation.13 | loop fusion | flops 6291456 | bytes 12582912 | tf_op jit(solution)/shard_map/transpose;reshape | solution.py:79
  6.6 52.6 %all_to_all.10 = bf16[4,1,128,2048]{3,2,1,0:T(8,128)(2,1)S(1)} all-to-all(bf16[4,1,128,2048]{3,2,1,0:T(8,128)(2,1)S(1)} %get-tuple-element.13), channel_id=1, replica_groups=mesh['shard'=4,'tensor'=4,'section'=2] {'shard'}, dimensions={0} | all-to-all | bytes 4194304 | tf_op jit(solution)/shard_map/all_to_all | solution.py:80
  59.2 1.7 %fusion.1 = f32[]{:T(128)} fusion(bf16[4,1,128,2048]{3,2,1,0:T(8,128)(2,1)S(1)} %all_to_all.10), kind=kLoop, calls=%fused_computation.5 | loop fusion | flops 3145727 | bytes 2097156 | tf_op jit(solution)/shard_map/reduce_sum | solution.py:27
  61.6 0.4 fusion.2
  62.0 0.0 copy-start.1
  62.0 1.3 copy-done.1
  63.3 1.3 fusion.52
  64.6 3.8 %add_convert_fusion.4 = bf16[512,2048]{1,0:T(8,128)(2,1)S(1)} fusion(bf16[512,2048]{1,0:T(8,128)(2,1)} %bitcast.30, f32[512,512]{1,0:T(8,128)S(1)} %fusion.52), kind=kOutput, calls=%fused_computation.12 | convolution fusion | flops 1347682304 | bytes 5242880 | tf_op jit(solution)/shard_map/kij,kjl->kil/dot_general | solution.py:41
  68.4 1.3 fusion.53
  69.6 2.9 %add_convert_fusion.3 = bf16[512,2048]{1,0:T(8,128)(2,1)} fusion(bf16[512,2048]{1,0:T(8,128)(2,1)S(1)} %add_convert_fusion.4, f32[512,512]{1,0:T(8,128)S(1)} %fusion.53), kind=kOutput, calls=%fused_computation.11 | convolution fusion | flops 1347682304 | bytes 5242880 | tf_op jit(solution)/shard_map/kij,kjl->kil/dot_general | solution.py:41
  72.5 0.0 copy-start.8
  72.5 3.7 %fusion.54 = f32[512,512]{1,0:T(8,128)S(1)} fusion(bf16[512,2048]{1,0:T(8,128)(2,1)} %add_convert_fusion.3), kind=kOutput, calls=%fused_computation.70 | convolution fusion | flops 1073741824 | bytes 3145728 | tf_op jit(solution)/shard_map/kij,klj->kil/dot_general | solution.py:34
  76.2 0.0 copy-done.8
  76.2 2.9 %add_convert_fusion.2 = bf16[512,2048]{1,0:T(8,128)(2,1)} fusion(bf16[512,2048]{1,0:T(8,128)(2,1)S(1)} %copy-done.8, f32[512,512]{1,0:T(8,128)S(1)} %fusion.54), kind=kOutput, calls=%fused_computation.10 | convolution fusion | flops 1347682304 | bytes 5242880 | tf_op jit(solution)/shard_map/kij,kjl->kil/dot_general | solution.py:41
  79.1 0.0 copy-start.9
  79.1 3.6 %fusion.55 = f32[512,512]{1,0:T(8,128)S(1)} fusion(bf16[512,2048]{1,0:T(8,128)(2,1)} %add_convert_fusion.2), kind=kOutput, calls=%fused_computation.71 | convolution fusion | flops 1073741824 | bytes 3145728 | tf_op jit(solution)/shard_map/kij,klj->kil/dot_general | solution.py:34
  82.7 0.0 copy-done.9
  82.8 2.9 %add_convert_fusion.1 = bf16[512,2048]{1,0:T(8,128)(2,1)} fusion(bf16[512,2048]{1,0:T(8,128)(2,1)S(1)} %copy-done.9, f32[512,512]{1,0:T(8,128)S(1)} %fusion.55), kind=kOutput, calls=%fused_computation.9 | convolution fusion | flops 1347682304 | bytes 5242880 | tf_op jit(solution)/shard_map/kij,kjl->kil/dot_general | solution.py:41
  85.6 0.0 copy-start.10
  85.6 3.6 %fusion.56 = f32[512,512]{1,0:T(8,128)S(1)} fusion(bf16[512,2048]{1,0:T(8,128)(2,1)} %add_convert_fusion.1), kind=kOutput, calls=%fused_computation.72 | convolution fusion | flops 1073741824 | bytes 3145728 | tf_op jit(solution)/shard_map/kij,klj->kil/dot_general | solution.py:34
  89.3 0.0 copy-done.10
  89.3 2.9 %add_convert_fusion = bf16[512,2048]{1,0:T(8,128)(2,1)} fusion(bf16[512,2048]{1,0:T(8,128)(2,1)S(1)} %copy-done.10, f32[512,512]{1,0:T(8,128)S(1)} %fusion.56), kind=kOutput, calls=%fused_computation.8 | convolution fusion | flops 1347682304 | bytes 5242880 | tf_op jit(solution)/shard_map/kij,kjl->kil/dot_general | solution.py:41
  92.2 0.0 copy-start.2
  92.2 0.0 copy-start.3
  92.2 0.0 copy-start.6
  92.2 0.0 copy-start.7
  92.2 0.0 copy-start.4
  92.2 0.0 copy-start.5
  92.2 3.8 %all-to-all-start.1 = ((bf16[4,1,128,2048]{3,2,1,0:T(8,128)(2,1)}), bf16[4,1,128,2048]{3,2,1,0:T(8,128)(2,1)S(1)}, u32[]{:S(2)}, u32[]{:S(2)}) async-start(bf16[4,1,128,2048]{3,2,1,0:T(8,128)(2,1)} %bitcast.28), calls=%async_computation.1 | async-start | bytes 4194304 | tf_op jit(solution)/shard_map/all_to_all | solution.py:84
  96.0 0.0 copy-done.2
  96.0 0.0 copy-done.3
  96.0 0.1 fusion.34
  96.1 0.0 copy-done
  96.1 0.0 copy-done.6
  96.1 0.0 copy-done.7
  96.1 0.2 convolution_bitcast_fusion
  96.3 61.1 %all-reduce = (f32[32,128]{1,0:T(8,128)S(1)}, f32[1,128]{1,0:T(1,128)S(1)}, f32[1,128]{1,0:T(1,128)S(1)}) all-reduce(f32[32,128]{1,0:T(8,128)S(1)} %convolution_bitcast_fusion, f32[1,128]{1,0:T(1,128)S(1)} %bitcast.32, f32[1,128]{1,0:T(1,128)S(1)} %bitcast.31), channel_id=1, replica_groups=mesh['shard'=4,'tensor'=4,'section'=2] {'shard','section'}, use_global_device_ids=true, to_apply=%region_5.6 | all-reduce | flops 4352 | bytes 34816 | tf_op jit(solution)/shard_map/psum | solution.py:70
  157.3 0.0 copy-done.4
  157.3 0.0 copy-done.5
  157.3 0.6 add_divide_fusion
  158.0 0.0 all-to-all-done.1
  158.0 2.6 %multiply_bitcast_fusion = f32[4,128,2048]{2,1,0:T(8,128)} fusion(bf16[4,1,128,2048]{3,2,1,0:T(8,128)(2,1)S(1)} %all-to-all-done.1), kind=kLoop, calls=%fused_computation.7 | loop fusion | flops 2097152 | bytes 6291456 | tf_op jit(solution)/shard_map/mul | solution.py:92
Async XLA Ops:
  0.6 95.5 %copy-start = (bf16[512,32]{0,1:T(8,128)(2,1)S(1)}, bf16[512,32]{0,1:T(8,128)(2,1)}, u32[]{:S(2)}) copy-start(bf16[512,32]{0,1:T(8,128)(2,1)} %param.15) | copy-start | bytes 98308
  62.0 1.3 copy-start.1
  72.5 3.7 %copy-start.8 = (bf16[512,2048]{1,0:T(8,128)(2,1)S(1)}, bf16[512,2048]{1,0:T(8,128)(2,1)}, u32[]{:S(2)}) copy-start(bf16[512,2048]{1,0:T(8,128)(2,1)} %add_convert_fusion.3) | copy-start | bytes 6291460
  79.1 3.7 %copy-start.9 = (bf16[512,2048]{1,0:T(8,128)(2,1)S(1)}, bf16[512,2048]{1,0:T(8,128)(2,1)}, u32[]{:S(2)}) copy-start(bf16[512,2048]{1,0:T(8,128)(2,1)} %add_convert_fusion.2) | copy-start | bytes 6291460
  85.6 3.7 %copy-start.10 = (bf16[512,2048]{1,0:T(8,128)(2,1)S(1)}, bf16[512,2048]{1,0:T(8,128)(2,1)}, u32[]{:S(2)}) copy-start(bf16[512,2048]{1,0:T(8,128)(2,1)} %add_convert_fusion.1) | copy-start | bytes 6291460
  92.2 3.8 %copy-start.2 = (bf16[512,128]{1,0:T(8,128)(2,1)S(1)}, bf16[512,128]{1,0:T(8,128)(2,1)}, u32[]{:S(2)}) copy-start(bf16[512,128]{1,0:T(8,128)(2,1)} %param.14) | copy-start | bytes 393220
  92.2 3.8 %copy-start.3 = (bf16[512,128]{1,0:T(8,128)(2,1)S(1)}, bf16[512,128]{1,0:T(8,128)(2,1)}, u32[]{:S(2)}) copy-start(bf16[512,128]{1,0:T(8,128)(2,1)} %param.11) | copy-start | bytes 393220
  92.2 3.9 %copy-start.6 = (f32[128]{0:T(128)S(1)}, f32[128]{0:T(128)}, u32[]{:S(2)}) copy-start(f32[128]{0:T(128)} %param.13) | copy-start | bytes 1540
  92.2 3.9 %copy-start.7 = (f32[128]{0:T(128)S(1)}, f32[128]{0:T(128)}, u32[]{:S(2)}) copy-start(f32[128]{0:T(128)} %param.12) | copy-start | bytes 1540
  92.2 65.1 %copy-start.4 = (f32[34,128]{1,0:T(8,128)S(1)}, f32[34,128]{1,0:T(8,128)}, u32[]{:S(2)}) copy-start(f32[34,128]{1,0:T(8,128)} %param.17) | copy-start | bytes 52228
  92.2 65.1 %copy-start.5 = (f32[34,128]{1,0:T(8,128)S(1)}, f32[34,128]{1,0:T(8,128)}, u32[]{:S(2)}) copy-start(f32[34,128]{1,0:T(8,128)} %param.16) | copy-start | bytes 52228
  92.2 65.8 %all-to-all-start.1 = ((bf16[4,1,128,2048]{3,2,1,0:T(8,128)(2,1)}), bf16[4,1,128,2048]{3,2,1,0:T(8,128)(2,1)S(1)}, u32[]{:S(2)}, u32[]{:S(2)}) async-start(bf16[4,1,128,2048]{3,2,1,0:T(8,128)(2,1)} %bitcast.28), calls=%async_computation.1 | async-start | bytes 4194304 | tf_op jit(solution)/shard_map/all_to_all | solution.py:84
where the time goes:
time: 163 us; the launch traced here: 161 us
  blocking collectives  114 us (70%)
  matrix products  29 us (18%)
  other arithmetic  11.4 us (7%)
  starting transfers between devices  3.75 us (2%)
    psum x1, blocking collectives, on_device(): lax.psum((gain_local, bias_local, router_local), ('shard', 'section'))  61.1 us
    all_to_all x1, blocking collectives, on_device(): lax.all_to_all(outgoing, 'shard', split_axis=0, concat_axis=0, tiled=True)  52.6 us
    dot_general x5, matrix products, orthogonalize(): jnp.einsum('kij,kjl->kil', poly, iterate, preferred_element_type=jnp.floa...  15.3 us
    dot_general x5, matrix products, orthogonalize(): jnp.einsum('kij,klj->kil', iterate, iterate, preferred_element_type=jnp.f...  13.5 us
    another operation x1, other arithmetic, on_device(): padded.reshape(slots, shard_count, rows_piece, cols_full)  5.98 us
    all_to_all x1, starting transfers between devices, on_device(): lax.all_to_all(result.reshape(items, shard_count, rows_piece, cols_full)....  3.75 us
  transfers between devices with their start and end apart: 1, of which 0 were waited for; matrix products, arithmetic and copies ran while one was open for 1% of the time, Pallas kernels for 0%

commit v1 on v0

--- a/solution.py
+++ b/solution.py
@@ -1,11 +1,16 @@
+import functools
 import math
 
 import jax
 import jax.numpy as jnp
 from jax import lax
+from jax.experimental import pallas as pl
+from jax.experimental.pallas import tpu as pltpu
 from jax.sharding import PartitionSpec as P
 
+D = 512
 FF = 2048
+EXPERTS = 32
 ITERS = 5
 
 
@@ -93,9 +98,269 @@
     return (next_momentum, update, next_first, next_second, adam_step)
 
 
+MESH = pl.DeviceIdType.MESH
+HALF = 24
+TILE = 512
+
+
+def ns_kernel(
+    n, grad_hbm, mom_hbm, vec_ref, back, vec_out, grad, mom, nest, mat, gram, half, poly,
+    vec_peer, vec_slots, load_sem, own_sem, in_send, in_recv, out_send, out_recv,
+    vs_send, vs_recv, vz_send, vz_recv, vf_send, vf_recv, gate,
+):
+    me = lax.axis_index("shard")
+    sec = lax.axis_index("section")
+    partner = {"section": 1 - sec}
+    rows, cols = nest.shape[1:]
+    d = n * rows
+    peers = [lax.rem(me + step, n) for step in range(1, n)]
+    sources = [lax.rem(me + n - step, n) for step in range(1, n)]
+    order = peers + [me]
+
+    def load(slot, k):
+        return (
+            pltpu.make_async_copy(grad_hbm.at[k], grad.at[slot], load_sem.at[0, slot]),
+            pltpu.make_async_copy(mom_hbm.at[k], mom.at[slot], load_sem.at[1, slot]),
+        )
+
+    for slot, k in enumerate(order):
+        for copy in load(slot, k):
+            copy.start()
+
+    barrier = pltpu.get_barrier_semaphore()
+    for peer in peers:
+        pl.semaphore_signal(barrier, inc=1, device_id={"shard": peer}, device_id_type=MESH)
+    pl.semaphore_signal(barrier, inc=1, device_id=partner, device_id_type=MESH)
+    pl.semaphore_wait(barrier, n)
+
+    def remote(src, dst, send, recv, where):
+        return pltpu.make_async_remote_copy(
+            src_ref=src, dst_ref=dst, send_sem=send, recv_sem=recv,
+            device_id=where, device_id_type=MESH,
+        )
+
+    def row_block(k):
+        return mat.at[pl.ds(pl.multiple_of(k * rows, rows), rows), :]
+
+    in_copies = [
+        remote(nest.at[j], row_block(me), in_send.at[j], in_recv.at[j], {"shard": peers[j]})
+        for j in range(n - 1)
+    ]
+    in_arrivals = [
+        remote(nest.at[j], row_block(sources[j]), in_send.at[j], in_recv.at[j], {"shard": peers[j]})
+        for j in range(n - 1)
+    ]
+    vec_swap = remote(vec_ref, vec_peer, vs_send, vs_recv, partner)
+    vec_swap.start()
+
+    for slot, k in enumerate(order):
+        for copy in load(slot, k):
+            copy.wait()
+        wide = grad[slot].astype(jnp.float32)
+        nest[slot] = (wide + MUON_DECAY * (MUON_DECAY * mom[slot] + wide)).astype(jnp.bfloat16)
+        if slot < n - 1:
+
+            @pl.when(sec == 0)
+            def _():
+                in_copies[slot].start()
+
+    own = pltpu.make_async_copy(nest.at[n - 1], row_block(me), own_sem.at[0])
+    own.start()
+
+    vec_swap.wait()
+    mine = pl.ds(pl.multiple_of(sec * HALF, HALF), HALF)
+    vec_slots[me] = vec_ref[mine, :] + vec_peer[mine, :]
+    vz = [
+        remote(vec_slots.at[me], vec_slots.at[me], vz_send.at[j], vz_recv.at[j], {"shard": peers[j]})
+        for j in range(n - 1)
+    ]
+    vz_arrivals = [
+        remote(
+            vec_slots.at[me], vec_slots.at[sources[j]], vz_send.at[j], vz_recv.at[j], {"shard": peers[j]}
+        )
+        for j in range(n - 1)
+    ]
+    for copy in vz:
+        copy.start()
+
+    @pl.when(sec == 1)
+    def _():
+        pl.semaphore_wait(gate, 1)
+        for copy in in_copies:
+            copy.start()
+
+    for copy in vz:
+        copy.wait_send()
+    for copy in vz_arrivals:
+        copy.wait_recv()
+    total = vec_slots[0]
+    for k in range(1, n):
+        total = total + vec_slots[k]
+    vec_out[mine, :] = total
+    final = remote(vec_out.at[mine, :], vec_out.at[mine, :], vf_send, vf_recv, partner)
+    theirs = pl.ds(pl.multiple_of((1 - sec) * HALF, HALF), HALF)
+    final_arrival = remote(vec_out.at[theirs, :], vec_out.at[theirs, :], vf_send, vf_recv, partner)
+    final.start()
+
+    for copy in in_copies:
+        copy.wait_send()
+
+    @pl.when(sec == 0)
+    def _():
+        pl.semaphore_signal(gate, inc=1, device_id=partner, device_id_type=MESH)
+
+    own.wait()
+    for copy in in_arrivals:
+        copy.wait_recv()
+
+    nt = (((1,), (1,)), ((), ()))
+    tiles = [slice(c, c + TILE) for c in range(0, cols, TILE)]
+
+    def add_gram(i, tile):
+        part = lax.dot_general(mat[:, tile], mat[:, tile], nt, preferred_element_type=jnp.float32)
+        if i == 0:
+            gram[...] = part
+        else:
+            gram[...] += part
+
+    for i, tile in enumerate(tiles):
+        add_gram(i, tile)
+    on_diagonal = lax.broadcasted_iota(jnp.int32, (d, d), 0) == lax.broadcasted_iota(
+        jnp.int32, (d, d), 1
+    )
+    trace = jnp.sum(jnp.where(on_diagonal, gram[...], 0.0))
+    scale = 1.0 / (jnp.sqrt(jnp.full((1, 1), trace, jnp.float32)) + NORM_EPSILON)
+
+    def step(repeat, scale):
+        wide = gram[...] * (scale * scale)
+        gram[...] = wide
+        half[...] = wide.astype(jnp.bfloat16)
+        square = jnp.dot(half[...], half[...], preferred_element_type=jnp.float32)
+        poly[...] = ((CUBIC_TERM * gram[...] + QUINTIC_TERM * square) * scale).astype(jnp.bfloat16)
+        linear = LINEAR_TERM * scale
+        for i, tile in enumerate(tiles):
+            now = mat[:, tile]
+            product = jnp.dot(poly[...], now, preferred_element_type=jnp.float32)
+            mat[:, tile] = (linear * now.astype(jnp.float32) + product).astype(jnp.bfloat16)
+            add_gram(i, tile)
+        return jnp.ones((1, 1), jnp.float32)
+
+    lax.fori_loop(0, ITERS, step, scale)
+
+    out_copies = [
+        remote(row_block(peers[j]), back.at[me], out_send.at[j], out_recv.at[j], {"shard": peers[j]})
+        for j in range(n - 1)
+    ]
+    out_arrivals = [
+        remote(
+            row_block(peers[j]), back.at[sources[j]], out_send.at[j], out_recv.at[j], {"shard": peers[j]}
+        )
+        for j in range(n - 1)
+    ]
+    for copy in out_copies:
+        copy.start()
+    keep = pltpu.make_async_copy(row_block(me), back.at[me], own_sem.at[1])
+    keep.start()
+    final.wait_send()
+    final_arrival.wait_recv()
+    keep.wait()
+    for copy in out_copies:
+        copy.wait_send()
+    for copy in out_arrivals:
+        copy.wait_recv()
+
+
+def fused(gradient, momentum, vec_local):
+    n, rows, cols = gradient.shape
+    d = n * rows
+    vmem = pl.BlockSpec(memory_space=pltpu.VMEM)
+    hbm = pl.BlockSpec(memory_space=pl.ANY)
+    dma = pltpu.SemaphoreType.DMA
+    return pl.pallas_call(
+        functools.partial(ns_kernel, n),
+        out_shape=(
+            jax.ShapeDtypeStruct((n, rows, cols), jnp.bfloat16),
+            jax.ShapeDtypeStruct(vec_local.shape, jnp.float32),
+        ),
+        in_specs=[hbm, hbm, vmem],
+        out_specs=(vmem, vmem),
+        scratch_shapes=[
+            pltpu.VMEM((n, rows, cols), jnp.bfloat16),
+            pltpu.VMEM((n, rows, cols), jnp.float32),
+            pltpu.VMEM((n, rows, cols), jnp.bfloat16),
+            pltpu.VMEM((d, cols), jnp.bfloat16),
+            pltpu.VMEM((d, d), jnp.float32),
+            pltpu.VMEM((d, d), jnp.bfloat16),
+            pltpu.VMEM((d, d), jnp.bfloat16),
+            pltpu.VMEM(vec_local.shape, jnp.float32),
+            pltpu.VMEM((n, HALF, vec_local.shape[1]), jnp.float32),
+            dma((2, n)),
+            dma((2,)),
+            dma((n - 1,)),
+            dma((n - 1,)),
+            dma((n - 1,)),
+            dma((n - 1,)),
+            dma,
+            dma,
+            dma((n - 1,)),
+            dma((n - 1,)),
+            dma,
+            dma,
+            pltpu.SemaphoreType.REGULAR,
+        ],
+        compiler_params=pltpu.CompilerParams(
+            collective_id=0, has_side_effects=True, vmem_limit_bytes=40 * 1024 * 1024
+        ),
+        cost_estimate=pl.CostEstimate(
+            flops=2 * ITERS * d * d * (2 * cols + d), bytes_accessed=8 * d * cols, transcendentals=0
+        ),
+    )(gradient, momentum, vec_local)
+
+
+def on_device_fused(
+    gradient,
+    momentum,
+    normed,
+    ln_gain,
+    ln_bias,
+    ln_cotangent,
+    router_cotangent,
+    first_moment,
+    second_moment,
+):
+    next_momentum = MUON_DECAY * momentum + gradient.astype(jnp.float32)
+    normed_float = normed.astype(jnp.float32)
+    cot_float = ln_cotangent.astype(jnp.float32)
+    ln_out = (ln_gain[None, :] * normed_float + ln_bias[None, :]).astype(jnp.bfloat16)
+    gain_local = jnp.sum(cot_float * normed_float, axis=0)
+    bias_local = jnp.sum(cot_float, axis=0)
+    router_local = lax.dot_general(
+        router_cotangent, ln_out, (((0,), (0,)), ((), ())), preferred_element_type=jnp.float32
+    )
+    vec_local = jnp.concatenate([gain_local[None, :], bias_local[None, :], router_local], axis=0)
+    vecs = vec_local.shape[0]
+    back, vec_sum = fused(gradient, momentum, jnp.pad(vec_local, ((0, 2 * HALF - vecs), (0, 0))))
+    vec_grad = vec_sum[:vecs]
+    next_first = ADAM_FIRST * first_moment + (1.0 - ADAM_FIRST) * vec_grad
+    next_second = ADAM_SECOND * second_moment + (1.0 - ADAM_SECOND) * vec_grad * vec_grad
+    adam_step = next_first / (jnp.sqrt(next_second) + ADAM_EPSILON)
+    update = back.astype(jnp.float32) * math.sqrt(FF)
+    return (next_momentum, update, next_first, next_second, adam_step)
+
+
+def takes_kernel(shape):
+    devices = shape["tensor"] * shape["section"]
+    return (
+        shape["section"] == 2
+        and EXPERTS == devices * shape["shard"]
+        and shape["shard"] > 1
+        and D % (128 * shape["shard"]) == 0
+    )
+
+
 def solution(mesh):
     return jax.shard_map(
-        on_device,
+        on_device_fused if takes_kernel(mesh.shape) else on_device,
         mesh=mesh,
         in_specs=(
             P(("tensor", "section"), "shard", None),

time: 163 us -> 124 us (0.76)
  the two profiles are of different devices: /device:TPU:1 before, /device:TPU:15 now
where the time goes in v1:
time: 124 us
  Pallas kernels  111 us (90%)
  other arithmetic  6.37 us (5%)
  local copies, waits for them, and re-layouts  4.55 us (4%)
    pallas_call x1, Pallas kernels, fused(): pl.pallas_call(functools.partial(ns_kernel, n), out_shape=(jax.ShapeDtype...  111 us
    mul x1, other arithmetic, on_device_fused(): update = back.astype(jnp.float32) * math.sqrt(FF)  4.68 us
    unnamed x14, local copies, waits for them, and re-layouts  4.55 us

profile of v1, /device:TPU:15, one launch (start us, length us, event | category | flops | bytes accessed | tf_op | source)
XLA Modules:
  0.0 123.6 jit_solution(3039360559417733990)
XLA Ops:
  0.6 0.0 copy-start
  0.6 0.7 copy-done
  1.4 1.1 convolution_bitcast_fusion
  2.5 1.1 fusion
  3.5 0.0 copy-start.1
  3.6 2.2 %copy-done.1 = f32[4,128,2048]{2,1,0:T(8,128)S(1)} copy-done((f32[4,128,2048]{2,1,0:T(8,128)S(1)}, f32[4,128,2048]{2,1,0:T(8,128)}, u32[]{:S(2)}) %copy-start.1) | copy-done | bytes 4194328
  5.7 0.0 copy-start.3
  5.7 1.6 %copy-done.3 = bf16[4,128,2048]{2,1,0:T(8,128)(2,1)S(1)} copy-done((bf16[4,128,2048]{2,1,0:T(8,128)(2,1)S(1)}, bf16[4,128,2048]{2,1,0:T(8,128)(2,1)}, u32[]{:S(2)}) %copy-start.3) | copy-done | bytes 2097176
  7.3 0.0 copy-start.2
  7.3 0.0 copy-start.4
  7.3 110.9 %shard_map.128 = (bf16[4,128,2048]{2,1,0:T(8,128)(2,1)S(1)}, f32[48,128]{1,0:T(8,128)S(1)}) custom-call(bf16[4,128,2048]{2,1,0:T(8,128)(2,1)S(1)} %copy-done.3, f32[4,128,2048]{2,1,0:T(8,128)S(1)} %copy-done.1, f32[48,128]{1,0:T(8,128)S(1)} %select_maximum_fusion.vec_ref), custom_call_target="tpu_custom_call" | custom-call | flops 12079595520 | bytes 8388608 | tf_op jit(solution)/shard_map/pallas_call | solution.py:279
  118.2 0.0 copy-done.2
  118.2 0.0 copy-done.4
  118.2 0.0 copy-start.5
  118.2 0.0 copy-start.6
  118.2 4.7 %convert_multiply_fusion = (f32[4,128,2048]{2,1,0:T(8,128)}, f32[4,128,2048]{2,1,0:T(8,128)}) fusion(bf16[4,128,2048]{2,1,0:T(8,128)(2,1)S(1)} %get-tuple-element.7, bf16[4,128,2048]{2,1,0:T(8,128)(2,1)S(1)} %copy-done.4, f32[4,128,2048]{2,1,0:T(8,128)S(1)} %copy-done.2), kind=kLoop, calls=%fused_computation | loop fusion | flops 5242880 | bytes 16777216 | tf_op jit(solution)/shard_map/mul | solution.py:347
  122.9 0.0 copy-done.5
  122.9 0.0 copy-done.6
  122.9 0.6 add_divide_fusion
  (1 shorter events, 0.0 us)
Async XLA Ops:
  0.6 0.8 copy-start
  3.5 2.2 %copy-start.1 = (f32[4,128,2048]{2,1,0:T(8,128)S(1)}, f32[4,128,2048]{2,1,0:T(8,128)}, u32[]{:S(2)}) copy-start(f32[4,128,2048]{2,1,0:T(8,128)} %mom_hbm.1) | copy-start | bytes 12582916
  5.7 1.6 %copy-start.3 = (bf16[4,128,2048]{2,1,0:T(8,128)(2,1)S(1)}, bf16[4,128,2048]{2,1,0:T(8,128)(2,1)}, u32[]{:S(2)}) copy-start(bf16[4,128,2048]{2,1,0:T(8,128)(2,1)} %grad_hbm.1) | copy-start | bytes 6291460
  7.3 110.9 %copy-start.2 = (f32[4,128,2048]{2,1,0:T(8,128)S(1)}, f32[4,128,2048]{2,1,0:T(8,128)}, u32[]{:S(2)}) copy-start(f32[4,128,2048]{2,1,0:T(8,128)} %mom_hbm.1) | copy-start | bytes 12582916
  7.3 110.9 %copy-start.4 = (bf16[4,128,2048]{2,1,0:T(8,128)(2,1)S(1)}, bf16[4,128,2048]{2,1,0:T(8,128)(2,1)}, u32[]{:S(2)}) copy-start(bf16[4,128,2048]{2,1,0:T(8,128)(2,1)} %grad_hbm.1) | copy-start | bytes 6291460
  118.2 4.7 %copy-start.5 = (f32[34,128]{1,0:T(8,128)S(1)}, f32[34,128]{1,0:T(8,128)}, u32[]{:S(2)}) copy-start(f32[34,128]{1,0:T(8,128)} %param.17) | copy-start | bytes 52228
  118.2 4.7 %copy-start.6 = (f32[34,128]{1,0:T(8,128)S(1)}, f32[34,128]{1,0:T(8,128)}, u32[]{:S(2)}) copy-start(f32[34,128]{1,0:T(8,128)} %param.16) | copy-start | bytes 52228

commit v2 on v1

--- a/solution.py
+++ b/solution.py
@@ -100,22 +100,35 @@
 
 MESH = pl.DeviceIdType.MESH
 HALF = 24
+CHUNKS = 1
+GATE = 1
 TILE = 512
 
 
+def flip(index, mask):
+    bit = 1
+    while bit <= mask:
+        if mask & bit:
+            index = index + bit * (1 - 2 * ((index // bit) % 2))
+        bit *= 2
+    return index
+
+
 def ns_kernel(
-    n, grad_hbm, mom_hbm, vec_ref, back, vec_out, grad, mom, nest, mat, gram, half, poly,
-    vec_peer, vec_slots, load_sem, own_sem, in_send, in_recv, out_send, out_recv,
-    vs_send, vs_recv, vz_send, vz_recv, vf_send, vf_recv, gate,
+    n, grad_hbm, mom_hbm, normed_hbm, cot_hbm, router_hbm, gain_ref, bias_ref, back, vec_out,
+    grad, mom, nest, mat, gram, half, poly, normed, cot, router, vec_ref,
+    vec_peer, vec_slots, load_sem, vec_sem, own_sem, in_send, in_recv, out_send, out_recv,
+    vs_send, vs_recv, vz_send, vz_recv, vf_send, vf_recv, gate, out_gate,
 ):
     me = lax.axis_index("shard")
     sec = lax.axis_index("section")
     partner = {"section": 1 - sec}
     rows, cols = nest.shape[1:]
     d = n * rows
-    peers = [lax.rem(me + step, n) for step in range(1, n)]
-    sources = [lax.rem(me + n - step, n) for step in range(1, n)]
+    peers = [flip(me, step) for step in range(n - 1, 0, -1)]
+    sources = peers
     order = peers + [me]
+    chunk = rows // CHUNKS
 
     def load(slot, k):
         return (
@@ -126,6 +139,13 @@
     for slot, k in enumerate(order):
         for copy in load(slot, k):
             copy.start()
+
+    vec_loads = [
+        pltpu.make_async_copy(src, dst, vec_sem.at[i])
+        for i, (src, dst) in enumerate(((normed_hbm, normed), (cot_hbm, cot), (router_hbm, router)))
+    ]
+    for copy in vec_loads:
+        copy.start()
 
     barrier = pltpu.get_barrier_semaphore()
     for peer in peers:
@@ -142,16 +162,15 @@
     def row_block(k):
         return mat.at[pl.ds(pl.multiple_of(k * rows, rows), rows), :]
 
-    in_copies = [
-        remote(nest.at[j], row_block(me), in_send.at[j], in_recv.at[j], {"shard": peers[j]})
-        for j in range(n - 1)
-    ]
-    in_arrivals = [
-        remote(nest.at[j], row_block(sources[j]), in_send.at[j], in_recv.at[j], {"shard": peers[j]})
-        for j in range(n - 1)
-    ]
-    vec_swap = remote(vec_ref, vec_peer, vs_send, vs_recv, partner)
-    vec_swap.start()
+    def in_copy(j, c, source):
+        return remote(
+            nest.at[j, pl.ds(c * chunk, chunk), :],
+            mat.at[pl.ds(pl.multiple_of(source * rows + c * chunk, chunk), chunk), :],
+            in_send.at[j, c], in_recv.at[j, c], {"shard": peers[j]},
+        )
+
+    pieces = [(j, c) for c in range(CHUNKS) for j in range(n // 2)]
+    pieces += [(j, c) for c in range(CHUNKS) for j in range(n // 2, n - 1)]
 
     for slot, k in enumerate(order):
         for copy in load(slot, k):
@@ -162,11 +181,27 @@
 
             @pl.when(sec == 0)
             def _():
-                in_copies[slot].start()
+                for c in range(CHUNKS):
+                    in_copy(slot, c, me).start()
 
     own = pltpu.make_async_copy(nest.at[n - 1], row_block(me), own_sem.at[0])
     own.start()
 
+    for copy in vec_loads:
+        copy.wait()
+    normed_wide = normed[...].astype(jnp.float32)
+    cot_wide = cot[...].astype(jnp.float32)
+    ln_out = (gain_ref[...] * normed_wide + bias_ref[...]).astype(jnp.bfloat16)
+    experts = router.shape[0]
+    vec_ref[0:experts, :] = jnp.dot(router[...], ln_out, preferred_element_type=jnp.float32)
+    gain_sum = jnp.sum(cot_wide * normed_wide, axis=0, keepdims=True)
+    bias_sum = jnp.sum(cot_wide, axis=0, keepdims=True)
+    rest = vec_ref.shape[0] - experts
+    row = lax.broadcasted_iota(jnp.int32, (rest, cot.shape[1]), 0)
+    vec_ref[experts:, :] = jnp.where(row == 0, gain_sum, jnp.where(row == 1, bias_sum, 0.0))
+
+    vec_swap = remote(vec_ref, vec_peer, vs_send, vs_recv, partner)
+    vec_swap.start()
     vec_swap.wait()
     mine = pl.ds(pl.multiple_of(sec * HALF, HALF), HALF)
     vec_slots[me] = vec_ref[mine, :] + vec_peer[mine, :]
@@ -186,8 +221,8 @@
     @pl.when(sec == 1)
     def _():
         pl.semaphore_wait(gate, 1)
-        for copy in in_copies:
-            copy.start()
+        for j, c in pieces:
+            in_copy(j, c, me).start()
 
     for copy in vz:
         copy.wait_send()
@@ -202,16 +237,22 @@
     final_arrival = remote(vec_out.at[theirs, :], vec_out.at[theirs, :], vf_send, vf_recv, partner)
     final.start()
 
-    for copy in in_copies:
-        copy.wait_send()
+    for j, c in pieces[:GATE]:
+        in_copy(j, c, peers[j]).wait_recv()
 
     @pl.when(sec == 0)
     def _():
         pl.semaphore_signal(gate, inc=1, device_id=partner, device_id_type=MESH)
 
+    for j, c in pieces[GATE:]:
+        in_copy(j, c, peers[j]).wait_recv()
+    for j, c in pieces:
+        in_copy(j, c, me).wait_send()
     own.wait()
-    for copy in in_arrivals:
-        copy.wait_recv()
+
+    @pl.when(sec == 1)
+    def _():
+        pl.semaphore_signal(out_gate, inc=1, device_id=partner, device_id_type=MESH)
 
     nt = (((1,), (1,)), ((), ()))
     tiles = [slice(c, c + TILE) for c in range(0, cols, TILE)]
@@ -257,6 +298,11 @@
         )
         for j in range(n - 1)
     ]
+
+    @pl.when(sec == 0)
+    def _():
+        pl.semaphore_wait(out_gate, 1)
+
     for copy in out_copies:
         copy.start()
     keep = pltpu.make_async_copy(row_block(me), back.at[me], own_sem.at[1])
@@ -270,19 +316,20 @@
         copy.wait_recv()
 
 
-def fused(gradient, momentum, vec_local):
+def fused(gradient, momentum, normed, cotangent, router, gain, bias):
     n, rows, cols = gradient.shape
     d = n * rows
+    sums = jax.ShapeDtypeStruct((2 * HALF, gain.shape[1]), jnp.float32)
     vmem = pl.BlockSpec(memory_space=pltpu.VMEM)
-    hbm = pl.BlockSpec(memory_space=pl.ANY)
+    hbm = pl.BlockSpec(memory_space=pltpu.HBM)
     dma = pltpu.SemaphoreType.DMA
     return pl.pallas_call(
         functools.partial(ns_kernel, n),
         out_shape=(
             jax.ShapeDtypeStruct((n, rows, cols), jnp.bfloat16),
-            jax.ShapeDtypeStruct(vec_local.shape, jnp.float32),
+            sums,
         ),
-        in_specs=[hbm, hbm, vmem],
+        in_specs=[hbm, hbm, hbm, hbm, hbm, vmem, vmem],
         out_specs=(vmem, vmem),
         scratch_shapes=[
             pltpu.VMEM((n, rows, cols), jnp.bfloat16),
@@ -292,12 +339,17 @@
             pltpu.VMEM((d, d), jnp.float32),
             pltpu.VMEM((d, d), jnp.bfloat16),
             pltpu.VMEM((d, d), jnp.bfloat16),
-            pltpu.VMEM(vec_local.shape, jnp.float32),
-            pltpu.VMEM((n, HALF, vec_local.shape[1]), jnp.float32),
+            pltpu.VMEM(normed.shape, jnp.bfloat16),
+            pltpu.VMEM(cotangent.shape, jnp.bfloat16),
+            pltpu.VMEM(router.shape, jnp.bfloat16),
+            pltpu.VMEM(sums.shape, jnp.float32),
+            pltpu.VMEM(sums.shape, jnp.float32),
+            pltpu.VMEM((n, HALF, sums.shape[1]), jnp.float32),
             dma((2, n)),
+            dma((3,)),
             dma((2,)),
-            dma((n - 1,)),
-            dma((n - 1,)),
+            dma((n - 1, CHUNKS)),
+            dma((n - 1, CHUNKS)),
             dma((n - 1,)),
             dma((n - 1,)),
             dma,
@@ -307,14 +359,15 @@
             dma,
             dma,
             pltpu.SemaphoreType.REGULAR,
+            pltpu.SemaphoreType.REGULAR,
         ],
         compiler_params=pltpu.CompilerParams(
-            collective_id=0, has_side_effects=True, vmem_limit_bytes=40 * 1024 * 1024
+            collective_id=0, has_side_effects=True, vmem_limit_bytes=60 * 1024 * 1024
         ),
         cost_estimate=pl.CostEstimate(
             flops=2 * ITERS * d * d * (2 * cols + d), bytes_accessed=8 * d * cols, transcendentals=0
         ),
-    )(gradient, momentum, vec_local)
+    )(gradient, momentum, normed, cotangent, router, gain, bias)
 
 
 def on_device_fused(
@@ -329,18 +382,11 @@
     second_moment,
 ):
     next_momentum = MUON_DECAY * momentum + gradient.astype(jnp.float32)
-    normed_float = normed.astype(jnp.float32)
-    cot_float = ln_cotangent.astype(jnp.float32)
-    ln_out = (ln_gain[None, :] * normed_float + ln_bias[None, :]).astype(jnp.bfloat16)
-    gain_local = jnp.sum(cot_float * normed_float, axis=0)
-    bias_local = jnp.sum(cot_float, axis=0)
-    router_local = lax.dot_general(
-        router_cotangent, ln_out, (((0,), (0,)), ((), ())), preferred_element_type=jnp.float32
-    )
-    vec_local = jnp.concatenate([gain_local[None, :], bias_local[None, :], router_local], axis=0)
-    vecs = vec_local.shape[0]
-    back, vec_sum = fused(gradient, momentum, jnp.pad(vec_local, ((0, 2 * HALF - vecs), (0, 0))))
-    vec_grad = vec_sum[:vecs]
+    back, vec_sum = fused(
+        gradient, momentum, normed, ln_cotangent, router_cotangent.T, ln_gain[None, :], ln_bias[None, :]
+    )
+    experts = router_cotangent.shape[1]
+    vec_grad = jnp.concatenate([vec_sum[experts : experts + 2], vec_sum[:experts]], axis=0)
     next_first = ADAM_FIRST * first_moment + (1.0 - ADAM_FIRST) * vec_grad
     next_second = ADAM_SECOND * second_moment + (1.0 - ADAM_SECOND) * vec_grad * vec_grad
     adam_step = next_first / (jnp.sqrt(next_second) + ADAM_EPSILON)
@@ -353,7 +399,7 @@
     return (
         shape["section"] == 2
         and EXPERTS == devices * shape["shard"]
-        and shape["shard"] > 1
+        and shape["shard"] in (2, 4)
         and D % (128 * shape["shard"]) == 0
     )
 

time: 124 us -> 113 us (0.911)
  the two profiles are of different devices: /device:TPU:15 before, /device:TPU:1 now
where the time goes in v2:
time: 113 us
  Pallas kernels  104 us (92%)
  other arithmetic  8.46 us (7%)
    pallas_call x1, Pallas kernels, fused(): pl.pallas_call(functools.partial(ns_kernel, n), out_shape=(jax.ShapeDtype...  104 us
    mul x1, other arithmetic, on_device_fused(): update = back.astype(jnp.float32) * math.sqrt(FF)  7.83 us

profile of v2, /device:TPU:1, one launch (start us, length us, event | category | flops | bytes accessed | tf_op | source)
XLA Modules:
  0.0 113.2 jit_solution(17623343503214961562)
XLA Ops:
  0.6 0.0 copy-start
  0.6 104.1 %shard_map.128 = (bf16[4,128,2048]{2,1,0:T(8,128)(2,1)}, f32[48,128]{1,0:T(8,128)}) custom-call(bf16[4,128,2048]{2,1,0:T(8,128)(2,1)} %grad_hbm.1, f32[4,128,2048]{2,1,0:T(8,128)} %mom_hbm.1, bf16[512,128]{1,0:T(8,128)(2,1)} %normed_hbm.1, bf16[512,128]{1,0:T(8,128)(2,1)} %cot_hbm.1, bf16[32,512]{1,0:T(8,128)(2,1)} %bitcast.3, f32[1,128]{1,0:T(1,128)} %bitcast.4, ...), custom_call_target="tpu_custom_call" | custom-call | flops 12079595520 | bytes 8388608 | tf_op jit(solution)/shard_map/pallas_call | solution.py:326
  104.7 0.0 copy-done
  104.7 0.0 copy-start.3
  104.7 0.0 copy-start.1
  104.7 0.0 copy-start.2
  104.8 7.8 %convert_multiply_fusion = (f32[4,128,2048]{2,1,0:T(8,128)}, f32[4,128,2048]{2,1,0:T(8,128)}) fusion(bf16[4,128,2048]{2,1,0:T(8,128)(2,1)} %get-tuple-element.7, bf16[4,128,2048]{2,1,0:T(8,128)(2,1)S(1)} %copy-done, f32[4,128,2048]{2,1,0:T(8,128)} %mom_hbm.1), kind=kLoop, calls=%fused_computation | loop fusion | flops 5242880 | bytes 16777216 | tf_op jit(solution)/shard_map/mul | solution.py:393
  112.6 0.0 copy-done.3
  112.6 0.0 copy-done.1
  112.6 0.0 copy-done.2
  112.6 0.6 add_divide_fusion
  (2 shorter events, 0.0 us)
Async XLA Ops:
  0.6 104.1 %copy-start = (bf16[4,128,2048]{2,1,0:T(8,128)(2,1)S(1)}, bf16[4,128,2048]{2,1,0:T(8,128)(2,1)}, u32[]{:S(2)}) copy-start(bf16[4,128,2048]{2,1,0:T(8,128)(2,1)} %grad_hbm.1) | copy-start | bytes 6291460
  104.7 7.9 %copy-start.3 = (f32[48,128]{1,0:T(8,128)S(1)}, f32[48,128]{1,0:T(8,128)}, u32[]{:S(2)}) copy-start(f32[48,128]{1,0:T(8,128)} %get-tuple-element.8) | copy-start | bytes 73732
  104.7 7.9 %copy-start.1 = (f32[34,128]{1,0:T(8,128)S(1)}, f32[34,128]{1,0:T(8,128)}, u32[]{:S(2)}) copy-start(f32[34,128]{1,0:T(8,128)} %param.17) | copy-start | bytes 52228
  104.7 7.9 %copy-start.2 = (f32[34,128]{1,0:T(8,128)S(1)}, f32[34,128]{1,0:T(8,128)}, u32[]{:S(2)}) copy-start(f32[34,128]{1,0:T(8,128)} %param.16) | copy-start | bytes 52228

commit v3 on v2

--- a/solution.py
+++ b/solution.py
@@ -115,8 +115,8 @@
 
 
 def ns_kernel(
-    n, grad_hbm, mom_hbm, normed_hbm, cot_hbm, router_hbm, gain_ref, bias_ref, back, vec_out,
-    grad, mom, nest, mat, gram, half, poly, normed, cot, router, vec_ref,
+    n, grad_hbm, mom_hbm, normed_hbm, cot_hbm, router_hbm, gain_ref, bias_ref, back, vec_out, mom,
+    grad, nest, mat, gram, half, poly, normed, cot, router, vec_ref,
     vec_peer, vec_slots, load_sem, vec_sem, own_sem, in_send, in_recv, out_send, out_recv,
     vs_send, vs_recv, vz_send, vz_recv, vf_send, vf_recv, gate, out_gate,
 ):
@@ -133,7 +133,7 @@
     def load(slot, k):
         return (
             pltpu.make_async_copy(grad_hbm.at[k], grad.at[slot], load_sem.at[0, slot]),
-            pltpu.make_async_copy(mom_hbm.at[k], mom.at[slot], load_sem.at[1, slot]),
+            pltpu.make_async_copy(mom_hbm.at[k], mom.at[k], load_sem.at[1, slot]),
         )
 
     for slot, k in enumerate(order):
@@ -176,7 +176,9 @@
         for copy in load(slot, k):
             copy.wait()
         wide = grad[slot].astype(jnp.float32)
-        nest[slot] = (wide + MUON_DECAY * (MUON_DECAY * mom[slot] + wide)).astype(jnp.bfloat16)
+        fresh = MUON_DECAY * mom[k] + wide
+        mom[k] = fresh
+        nest[slot] = (wide + MUON_DECAY * fresh).astype(jnp.bfloat16)
         if slot < n - 1:
 
             @pl.when(sec == 0)
@@ -328,12 +330,12 @@
         out_shape=(
             jax.ShapeDtypeStruct((n, rows, cols), jnp.bfloat16),
             sums,
+            jax.ShapeDtypeStruct((n, rows, cols), jnp.float32),
         ),
         in_specs=[hbm, hbm, hbm, hbm, hbm, vmem, vmem],
-        out_specs=(vmem, vmem),
+        out_specs=(vmem, vmem, vmem),
         scratch_shapes=[
             pltpu.VMEM((n, rows, cols), jnp.bfloat16),
-            pltpu.VMEM((n, rows, cols), jnp.float32),
             pltpu.VMEM((n, rows, cols), jnp.bfloat16),
             pltpu.VMEM((d, cols), jnp.bfloat16),
             pltpu.VMEM((d, d), jnp.float32),
@@ -362,12 +364,46 @@
             pltpu.SemaphoreType.REGULAR,
         ],
         compiler_params=pltpu.CompilerParams(
-            collective_id=0, has_side_effects=True, vmem_limit_bytes=60 * 1024 * 1024
+            collective_id=0, has_side_effects=True, vmem_limit_bytes=40 * 1024 * 1024
         ),
         cost_estimate=pl.CostEstimate(
             flops=2 * ITERS * d * d * (2 * cols + d), bytes_accessed=8 * d * cols, transcendentals=0
         ),
     )(gradient, momentum, normed, cotangent, router, gain, bias)
+
+
+def finish_kernel(fresh, back, moment_hbm, update_hbm, wide, moment_sem, update_sem):
+    n = back.shape[0]
+    moments = [
+        pltpu.make_async_copy(fresh.at[k], moment_hbm.at[k], moment_sem.at[k]) for k in range(n)
+    ]
+    updates = [
+        pltpu.make_async_copy(wide.at[k], update_hbm.at[k], update_sem.at[k]) for k in range(n)
+    ]
+    for k in range(n):
+        moments[k].start()
+        wide[k] = back[k].astype(jnp.float32) * math.sqrt(FF)
+        updates[k].start()
+    for copy in moments + updates:
+        copy.wait()
+
+
+def finish(fresh, back):
+    n = back.shape[0]
+    result = jax.ShapeDtypeStruct(back.shape, jnp.float32)
+    hbm = pl.BlockSpec(memory_space=pltpu.HBM)
+    return pl.pallas_call(
+        finish_kernel,
+        out_shape=(result, result),
+        in_specs=[pl.BlockSpec(memory_space=pltpu.VMEM)] * 2,
+        out_specs=(hbm, hbm),
+        scratch_shapes=[
+            pltpu.VMEM(back.shape, jnp.float32),
+            pltpu.SemaphoreType.DMA((n,)),
+            pltpu.SemaphoreType.DMA((n,)),
+        ],
+        compiler_params=pltpu.CompilerParams(vmem_limit_bytes=40 * 1024 * 1024),
+    )(fresh, back)
 
 
 def on_device_fused(
@@ -381,8 +417,7 @@
     first_moment,
     second_moment,
 ):
-    next_momentum = MUON_DECAY * momentum + gradient.astype(jnp.float32)
-    back, vec_sum = fused(
+    back, vec_sum, fresh = fused(
         gradient, momentum, normed, ln_cotangent, router_cotangent.T, ln_gain[None, :], ln_bias[None, :]
     )
     experts = router_cotangent.shape[1]
@@ -390,7 +425,7 @@
     next_first = ADAM_FIRST * first_moment + (1.0 - ADAM_FIRST) * vec_grad
     next_second = ADAM_SECOND * second_moment + (1.0 - ADAM_SECOND) * vec_grad * vec_grad
     adam_step = next_first / (jnp.sqrt(next_second) + ADAM_EPSILON)
-    update = back.astype(jnp.float32) * math.sqrt(FF)
+    next_momentum, update = finish(fresh, back)
     return (next_momentum, update, next_first, next_second, adam_step)
 
 

time: 113 us -> 115 us (1.018)
  other arithmetic: 8.46 us -> 0.64 us
  local copies, waits for them, and re-layouts: 0.02 us -> 7.66 us
  Pallas kernels: 104 us -> 106 us
    mul x1 -> x0, other arithmetic: 7.83 us -> none  [on_device_fused(): update = back.astype(jnp.float32) * math.sqrt(FF)]
    unnamed x8 -> x18, local copies, waits for them, and re-layouts: 0.02 us -> 7.66 us
    pallas_call x0 -> x1, Pallas kernels: none -> 3.37 us  [finish(): pl.pallas_call(finish_kernel, out_shape=(result, result), in_specs=[pl.Bl...]
    pallas_call x1, Pallas kernels: 104 us -> 103 us  [fused(): pl.pallas_call(functools.partial(ns_kernel, n), out_shape=(jax.ShapeDtype...]
where the time goes in v3:
time: 115 us
  Pallas kernels  106 us (92%)
  local copies, waits for them, and re-layouts  7.66 us (7%)
    pallas_call x1, Pallas kernels, fused(): pl.pallas_call(functools.partial(ns_kernel, n), out_shape=(jax.ShapeDtype...  103 us
    unnamed x18, local copies, waits for them, and re-layouts  7.66 us
    pallas_call x1, Pallas kernels, finish(): pl.pallas_call(finish_kernel, out_shape=(result, result), in_specs=[pl.Bl...  3.37 us

profile of v3, /device:TPU:1, one launch (start us, length us, event | category | flops | bytes accessed | tf_op | source)
XLA Modules:
  0.0 115.1 jit_solution(9456197531457162955)
XLA Ops:
  0.6 0.0 copy-start
  0.6 2.2 %copy-done = f32[4,128,2048]{2,1,0:T(8,128)S(1)} copy-done((f32[4,128,2048]{2,1,0:T(8,128)S(1)}, f32[4,128,2048]{2,1,0:T(8,128)}, u32[]{:S(2)}) %copy-start) | copy-done | bytes 4194328
  2.8 0.0 copy-start.1
  2.8 1.6 %copy-done.1 = bf16[4,128,2048]{2,1,0:T(8,128)(2,1)S(1)} copy-done((bf16[4,128,2048]{2,1,0:T(8,128)(2,1)S(1)}, bf16[4,128,2048]{2,1,0:T(8,128)(2,1)}, u32[]{:S(2)}) %copy-start.1) | copy-done | bytes 2097176
  4.4 0.0 copy-start.2
  4.4 0.9 copy-done.2
  5.3 0.0 copy-start.3
  5.3 0.9 copy-done.3
  6.2 0.0 copy-start.4
  6.2 0.8 copy-done.4
  7.0 0.0 copy-start.5
  7.0 0.7 copy-done.5
  7.6 0.0 copy-start.6
  7.6 0.7 copy-done.6
  8.3 102.7 %shard_map.128 = (bf16[4,128,2048]{2,1,0:T(8,128)(2,1)S(1)}, f32[48,128]{1,0:T(8,128)S(1)}, f32[4,128,2048]{2,1,0:T(8,128)S(1)}) custom-call(bf16[4,128,2048]{2,1,0:T(8,128)(2,1)S(1)} %copy-done.1, f32[4,128,2048]{2,1,0:T(8,128)S(1)} %copy-done, bf16[512,128]{1,0:T(8,128)(2,1)S(1)} %copy-done.2, bf16[512,128]{1,0:T(8,128)(2,1)S(1)} %copy-done.3, ...), custom_call_target="tpu_custom_call" | custom-call | flops 12079595520 | bytes 8388608 | tf_op jit(solution)/shard_map/pallas_call | solution.py:328
  111.0 0.0 copy-start.7
  111.0 0.0 copy-start.8
  111.1 3.4 %shard_map.129 = (f32[4,128,2048]{2,1,0:T(8,128)}, f32[4,128,2048]{2,1,0:T(8,128)}) custom-call(f32[4,128,2048]{2,1,0:T(8,128)S(1)} %get-tuple-element.10.fresh, bf16[4,128,2048]{2,1,0:T(8,128)(2,1)S(1)} %get-tuple-element.11.back), custom_call_target="tpu_custom_call" | custom-call | tf_op jit(solution)/shard_map/pallas_call | solution.py:395
  114.5 0.0 copy-done.7
  114.5 0.0 copy-done.8
  114.5 0.6 add_divide_fusion
  (2 shorter events, 0.0 us)
Async XLA Ops:
  0.6 2.2 %copy-start = (f32[4,128,2048]{2,1,0:T(8,128)S(1)}, f32[4,128,2048]{2,1,0:T(8,128)}, u32[]{:S(2)}) copy-start(f32[4,128,2048]{2,1,0:T(8,128)} %mom_hbm.1) | copy-start | bytes 12582916
  2.8 1.6 %copy-start.1 = (bf16[4,128,2048]{2,1,0:T(8,128)(2,1)S(1)}, bf16[4,128,2048]{2,1,0:T(8,128)(2,1)}, u32[]{:S(2)}) copy-start(bf16[4,128,2048]{2,1,0:T(8,128)(2,1)} %grad_hbm.1) | copy-start | bytes 6291460
  4.4 0.9 copy-start.2
  5.3 0.9 copy-start.3
  6.2 0.8 copy-start.4
  7.0 0.7 copy-start.5
  7.6 0.7 copy-start.6
  111.0 3.4 %copy-start.7 = (f32[34,128]{1,0:T(8,128)S(1)}, f32[34,128]{1,0:T(8,128)}, u32[]{:S(2)}) copy-start(f32[34,128]{1,0:T(8,128)} %param.17) | copy-start | bytes 52228
  111.0 3.4 %copy-start.8 = (f32[34,128]{1,0:T(8,128)S(1)}, f32[34,128]{1,0:T(8,128)}, u32[]{:S(2)}) copy-start(f32[34,128]{1,0:T(8,128)} %param.16) | copy-start | bytes 52228
